TPU v7x, 32 devices: a whole 2x2x4 slice. The times are simulated.
32 devices in a mesh: section: 2 (over core), batch: 16 (over z, y, x).
Axes of the slice: x: 2, y: 2, z: 4, core: 2. Of those that a mesh axis runs over, the one named last changes fastest.
Arguments:
- frames: bfloat16 [2, 24, 384, 2000], P(None, None, 'batch', 'section'), may hold values from -6 to 6
- grad_out: bfloat16 [2, 24, 384, 2000], P(None, None, 'batch', 'section'), may hold values from -6 to 6
- weights: bfloat16 [2, 2000, 2000], P('section'), may hold values from -0.125 to 0.125
- gains: float32 [2, 2000], P('section'), may hold values from 0.5 to 1.5
- shifts: float32 [2, 2000], P('section'), may hold values from -1 to 1
- recurs: float32 [2, 2000], P('section'), may hold values from 0.05 to 0.95
- lengths: int32 [2, 128], P(None, 'batch'), may hold values from 1 to 24, 1920 in all within a row
- masks: int32 [2, 24, 384], P(None, None, 'batch'), may hold values 0 or 1
Outputs:
- grad_frames: bfloat16 [2, 24, 384, 2000], P(None, None, 'batch', 'section')
- grad_weights: float32 [2, 2000, 2000], P('section')
- grad_gains: float32 [2, 2000], P('section')
- grad_shifts: float32 [2, 2000], P('section')
- grad_recurs: float32 [2, 2000], P('section')
- rms_table: float32 [2, 2], P('section')
Inputs may be any that keep to these rules, and one draw needn't show every extreme that they name: `lengths`: each micro-batch has a group of 24 frames.
All inputs are finite; a program needn't handle non-finite values. No bound on the sum of `masks` on one device may be relied on, other than what follows from the above.
Results may differ from a plain program's by a relative error of at most 0.007.
Values may be sent and summed in bfloat16 or wider, within the bound.
A program may use at most 256 MiB of HBM per device.

v0:
```python
import functools

import jax
import jax.numpy as jnp
from jax import lax
from jax.experimental import pallas as pl
from jax.experimental.pallas import tpu as pltpu
from jax.sharding import PartitionSpec as P

EPS = 1e-05
W = 1024
HALF = W // 2
QUART = W // 4
MESH = pl.DeviceIdType.MESH
F32 = jnp.float32
BF16 = jnp.bfloat16


def grid_of(size):
    if size == 16:
        return (4, 2, 2)
    if size == 128:
        return (8, 4, 4)
    return (size, 1, 1)


def aligned(x, k):
    return pl.multiple_of(x, k)


def wide(x, reps):
    return jnp.concatenate([x] * reps, axis=1)


def fold(x):
    rows = x.shape[0]
    total = x[0:8]
    for k in range(8, rows, 8):
        total = total + x[k : k + 8]
    return total


def dot(a, b, dims):
    return lax.dot_general(a, b, (dims, ((), ())), preferred_element_type=F32)


class Reduction:
    def __init__(self, env, layer, index, block, orders, lane_of):
        self.env, self.layer, self.index, self.block, self.orders = env, layer, index, block, orders
        self.lane_of = lane_of
        self.space = env["space"].at[layer, index]
        self.depth = len(orders[0])
        self.regions = [self.halves(i, order) for i, order in enumerate(orders)]
        self.step = 0
        self.waits = []
        depth = self.depth
        self.steps = [functools.partial(self.scatter, 0)]
        self.steps += [functools.partial(self.scatter, k) for k in range(1, depth)]
        self.steps += [functools.partial(self.gather, k) for k in range(depth - 1, 0, -1)]
        self.steps += [self.give, self.finish]

    def halves(self, i, order):
        row, rows, lane, lanes = 0, W, i * QUART, QUART
        out = [(row, rows, lane, lanes)]
        for axis in order:
            if rows > 16:
                rows //= 2
                row = row + axis["bit"] * rows
            else:
                lanes //= 2
                lane = lane + axis["bit"] * lanes
            out.append((row, rows, lane, lanes))
        return out

    @property
    def free_to_go(self):
        return self.step != self.depth or self.layer in self.env["summed"]

    @property
    def done(self):
        return self.step >= len(self.steps)

    def advance(self):
        self.sent = []
        self.steps[self.step]()
        self.step += 1
        return self.sent

    def remote(self, i, src, dst, slot, where, recv=None):
        sems = (self.layer, self.index, i, slot)
        return pltpu.make_async_remote_copy(
            src_ref=src, dst_ref=dst, send_sem=self.env["ar_send"].at[sems],
            recv_sem=self.env["ar_recv"].at[sems] if recv is None else recv, device_id=where, device_id_type=MESH,
        )

    def wait(self):
        for made, came in self.waits:
            made.wait_send()
            came.wait_recv()
        self.waits = []

    def came_at(self, i, k):
        row = sum(r[1] for r in self.regions[i][1 : k + 1])
        _, rows, _, lanes = self.regions[i][k + 1]
        return row, rows, i * QUART, lanes

    def scatter(self, k):
        if k > 0:
            self.wait()
            self.add(k - 1)
        for i, order in enumerate(self.orders):
            self.scatter_part(i, k, order[k])

    def start_part(self, i):
        self.sent = []
        self.scatter_part(i, 0, self.orders[i][0])
        if i == 1:
            self.step = 1
        return self.sent

    def scatter_part(self, i, k, axis):
        row, rows, lane, lanes = self.regions[i][k]
        _, rows2, _, lanes2 = self.regions[i][k + 1]
        give_row = row + (1 - axis["bit"]) * rows2 if rows2 < rows else row
        give_lane = lane if rows2 < rows else lane + (1 - axis["bit"]) * lanes2
        src = self.block.at[pl.ds(aligned(give_row, 16), rows2), pl.ds(aligned(give_lane, 128), lanes2)]
        at, n, at_lane, n_lanes = self.came_at(i, k)
        dst = self.space.at[pl.ds(at, n), pl.ds(at_lane, n_lanes)]
        made = self.remote(i, src, dst, k, axis["partner"])
        made.start()
        self.waits.append((made, made))
        self.sent.append((axis["link"], rows2 * lanes2 * 2))

    def add(self, k, last=False):
        rows = self.regions[0][k + 1][1]
        size = min(rows, 32)
        out = []
        for i in range(2):
            row, _, lane, lanes = self.regions[i][k + 1]
            at, _, at_lane, _ = self.came_at(i, k)
            lane = aligned(lane, 128)
            extra = None
            if last:
                part = self.index // 2
                first = aligned((self.index % 2) * HALF + lane, 128)
                extra = self.env["vtot"][self.layer, part : part + 1, pl.ds(first, lanes)]
            out.append((row, lane, lanes, at, at_lane, self.local(i, k + 1)[0], extra))

        def body(j, _):
            for row, lane, lanes, at, at_lane, home, extra in out:
                here = pl.ds(aligned(row + j * size, 16), size)
                total = self.block[here, pl.ds(lane, lanes)].astype(F32)
                total = total + self.space[pl.ds(aligned(at + j * size, 16), size), pl.ds(at_lane, lanes)].astype(F32)
                if last:
                    column = self.env["column"][self.layer, here, :].astype(F32)
                    total = total + wide(column, lanes // 128) * extra
                    to = pl.ds(aligned(home + j * size, 16), size)
                    self.space[to, pl.ds(lane, lanes)] = total.astype(BF16)
                else:
                    self.block[here, pl.ds(lane, lanes)] = total.astype(BF16)
            return 0

        lax.fori_loop(0, rows // size, body, 0)

    def local(self, i, k):
        row, rows, lane, lanes = self.regions[i][k]
        return row - self.regions[i][1][0], rows, lane, lanes

    def gather(self, k):
        self.wait()
        if k == self.depth - 1:
            self.add(k, last=True)
        for i, order in enumerate(self.orders):
            axis = order[k]
            row, rows, lane, lanes = self.local(i, k + 1)
            row0, rows0, lane0, lanes0 = self.local(i, k)
            if rows0 > rows:
                far = (row0 + (1 - axis["bit"]) * rows, rows, lane, lanes)
            else:
                far = (row, rows, lane0 + (1 - axis["bit"]) * lanes, lanes)
            refs = [
                self.space.at[pl.ds(aligned(r, 16), n), pl.ds(aligned(c, 128), w)]
                for r, n, c, w in ((row, rows, lane, lanes), far)
            ]
            made = self.remote(i, refs[0], refs[0], self.depth + k, axis["partner"])
            made.start()
            self.waits.append((made, self.remote(i, refs[1], refs[1], self.depth + k, axis["partner"])))
            self.sent.append((axis["link"], rows * lanes * 2))

    def result(self, i, bit, section):
        rows = self.regions[i][1][1]
        lane = aligned(self.lane_of(section) + i * QUART, QUART)
        return self.env["o"].at[section, pl.ds(aligned(bit * rows, 16), rows), pl.ds(lane, QUART)]

    def gathered(self, i):
        return self.space.at[pl.ds(0, self.regions[i][1][1]), pl.ds(i * QUART, QUART)]

    def deliver(self, i, near, straight):
        axis, section = self.orders[i][0], self.env["section"]
        slot = 2 * self.depth + (0 if near else 1)
        recv = None if straight else self.env["ar_other"].at[self.layer, self.index, i, 0 if near else 1]
        where = dict(self.env["here"] if near else axis["partner"], section=self.layer)
        return self.remote(i, self.gathered(i), self.result(i, axis["bit"], section), slot, where, recv)

    def arrival(self, i, near, straight):
        axis, section = self.orders[i][0], self.env["section"]
        slot = 2 * self.depth + (0 if near else 1)
        recv = None if straight else self.env["ar_other"].at[self.layer, self.index, i, 0 if near else 1]
        bit = axis["bit"] if near else 1 - axis["bit"]
        frm = section if straight else 1 - section
        where = dict(self.env["here"] if near else axis["partner"], section=frm)
        return self.remote(i, self.gathered(i), self.result(i, bit, frm), slot, where, recv)

    def kept(self, i):
        sem = self.env["ar_recv"].at[self.layer, self.index, i, 2 * self.depth]
        return pltpu.make_async_copy(
            self.gathered(i), self.result(i, self.orders[i][0]["bit"], self.env["section"]), sem
        )

    def give(self):
        self.wait()

        @pl.when(self.env["section"] == self.layer)
        def _():
            for i in range(2):
                self.deliver(i, False, True).start()
                self.kept(i).start()

        @pl.when(self.env["section"] != self.layer)
        def _():
            for i in range(2):
                self.deliver(i, False, False).start()
                self.deliver(i, True, False).start()

        for i, order in enumerate(self.orders):
            self.sent.append((order[0]["link"], self.regions[i][1][1] * QUART * 2))

    def finish(self):
        @pl.when(self.env["section"] == self.layer)
        def _():
            for i in range(2):
                self.kept(i).wait()
                self.deliver(i, False, True).wait_send()
                self.arrival(i, False, True).wait_recv()
                self.arrival(i, True, False).wait_recv()
                self.arrival(i, False, False).wait_recv()

        @pl.when(self.env["section"] != self.layer)
        def _():
            for i in range(2):
                self.deliver(i, False, False).wait_send()
                self.deliver(i, True, False).wait_send()


class Order:
    RATE, HOP = 50e3, 1.8

    def __init__(self):
        self.now = 0.0
        self.free = {}
        self.going = []

    def sent(self, copies):
        end = self.now
        for link, size in copies:
            self.free[link] = max(self.now, self.free.get(link, 0.0)) + size / self.RATE
            end = max(end, self.free[link])
        return end + self.HOP

    def begin(self, one, i):
        end = self.sent(one.start_part(i))
        if i == 0:
            one.due = end
        else:
            one.due = max(one.due, end)
            self.going.append(one)

    def advance(self, one):
        self.now = max(self.now, one.due) + 0.4
        one.due = self.sent(one.advance())
        if one.done:
            self.going.remove(one)

    def work(self, cost):
        self.now += cost
        while True:
            due = [x for x in self.going if x.due <= self.now and x.free_to_go]
            if not due:
                return
            self.advance(min(due, key=lambda x: x.due))

    def drain(self):
        while self.going:
            self.advance(min(self.going, key=lambda x: x.due))


def kernel(dims, steps, seqs, views, frames, grad_out, weights, gains, shifts, recurs, lengths, masks, o, gf, vectors, f_own, f_far, p_own, p_far, g3, wc, wr1, src_t, live, turn,
           staged, heads, tails, v, vecs, rows, hid, coef, tot, vtot, levels, column, counts, cnt_p, cnt_z, slim_p, slim_z,
           wide_p, wide_z, space, sems, v_sems, stage_sem, credit, pl_send, pl_recv, z_send, z_recv, ar_send, ar_recv,
           ar_other):
    nz, ny, nx = dims
    np_ = ny * nx
    span = steps * seqs
    total_rows = 2 * span
    sent_rows = total_rows + 16
    pairs = steps // 2
    section = lax.axis_index("section")
    other = 1 - section
    b = lax.axis_index("batch")
    mp = lax.rem(b, np_)
    mz = b // np_

    def at_plane(i):
        return {"batch": b - mp + i}

    def at_z(i):
        return {"batch": b + (i - mz) * np_}

    bits = []
    for link, count, stride in (("x", nx, 1), ("y", ny, nx), ("z", nz, np_)):
        while count > 1:
            bit = lax.rem(b // stride, 2)
            bits.append(dict(bit=bit, partner={"batch": b + (1 - 2 * bit) * stride}, link=link))
            count //= 2
            stride *= 2
    sibling = {"section": other}

    def local(src, dst, slot):
        return pltpu.make_async_copy(src, dst, sems.at[0, slot])

    def across(src, dst, slot):
        return pltpu.make_async_remote_copy(
            src_ref=src, dst_ref=dst, send_sem=sems.at[1, slot], recv_sem=sems.at[2, slot],
            device_id=sibling, device_id_type=MESH,
        )

    half = frames.shape[3]
    width = 2 * half
    lead = W - half
    rest = width - W
    full = rest // 128 * 128

    def fetch(source, m):
        return pltpu.make_async_copy(source.at[m], staged.at[m], stage_sem.at[m])

    def by_units(source, target, m):
        fetch(source, m).wait()

        @pl.when(section == 0)
        def _():
            def place(i, _):
                x = staged[m, pl.ds(2 * i, 2)].astype(F32).reshape(2 * seqs, half)
                head = heads[m, pl.ds(2 * i, 2)].astype(F32).reshape(2 * seqs, 128)
                to = pl.ds(aligned(m * span + 2 * i * seqs, 16), 2 * seqs)
                target[to, :] = jnp.concatenate([x, head[:, :lead]], axis=1).astype(BF16)
                return 0

            lax.fori_loop(0, pairs, place, 0)

        @pl.when(section == 1)
        def _():
            pad = jnp.zeros((2 * seqs, 2 * lead), F32)

            def place(i, _):
                x = staged[m, pl.ds(2 * i, 2)].astype(F32).reshape(2 * seqs, half)
                to = pl.ds(aligned(m * span + 2 * i * seqs, 16), 2 * seqs)
                target[to, :] = jnp.concatenate([x[:, lead:], pad], axis=1).astype(BF16)
                return 0

            lax.fori_loop(0, pairs, place, 0)

    def pieces(row, count, u, block, spot):
        r = pl.ds(row, count)
        to = pl.ds(0, count)
        if u == 0:
            return [(weights.at[0, r, pl.ds(0, W)], block.at[to, :])]
        return [
            (weights.at[0, r, pl.ds(W, full)], block.at[to, pl.ds(0, full)]),
            (weights.at[0, r, pl.ds(W + full, rest - full)], tails.at[spot, to, :]),
        ]

    rows_of = {0: (0, W), 1: (W, rest)}

    def w_plan(layer):
        mine, far = rows_of[layer], rows_of[1 - layer]
        plan = [
            (mine, layer, far, 1 - layer, wc.at[layer, 0], 2 * layer),
            (far, layer, mine, 1 - layer, wc.at[layer, 1], 2 * layer + 1),
        ]
        if layer == 1:
            plan.append((mine, 0, far, 1, wr1, 4))
        return plan

    late_row = (width - half) // 16 * 16
    late_shift = half - late_row
    late_plan = [
        ((0, W), 0, (late_row, width - late_row), 1, wc.at[0, 0], 0),
        ((0, W), 1, (late_row, width - late_row), 0, wc.at[0, 1], 1),
    ]
    slot_of = {0: 4, 1: 8, 2: 14}

    def local_w(plan, base, which):
        r, u, _, _, block, spot = plan[which]
        return [local(a, t, base + 2 * which + i) for i, (a, t) in enumerate(pieces(*r, u, block, spot))]

    def across_w(plan, base, which):
        _, _, r, u, block, spot = plan[which]
        return [across(a, t, base + 2 * which + i) for i, (a, t) in enumerate(pieces(*r, u, block, spot))]

    def start_local_w(layer, plan, base):
        @pl.when(section == layer)
        def _():
            for which in range(len(plan)):
                for made in local_w(plan, base, which):
                    made.start()

    def start_across_w(layer, plan, base):
        @pl.when(section == layer)
        def _():
            for which in range(len(plan)):
                for made in across_w(plan, base, which):
                    made.start()

    def last_units(block, spot):
        def body(i, _):
            r = pl.ds(aligned(i * 128, 128), 128)
            x = tails[spot, r, :].astype(F32)
            x = jnp.concatenate([x, jnp.zeros((128, 128 - x.shape[1]), F32)], axis=1)
            block[r, full:] = x.astype(BF16)
            return 0

        lax.fori_loop(0, W // 128, body, 0)

    def wait_w(layer, plan, base, which):
        _, own_u, _, far_u, block, spot = plan[which]

        @pl.when(section == layer)
        def _():
            for made in local_w(plan, base, which):
                made.wait()
            if own_u == 1:
                last_units(block, spot)

        @pl.when(section != layer)
        def _():
            for made in across_w(plan, base, which):
                made.wait_recv()
            if far_u == 1:
                last_units(block, spot)

    def done_w(layer, plan, base):
        @pl.when(section == layer)
        def _():
            for which in range(len(plan)):
                for made in across_w(plan, base, which):
                    made.wait_send()

    def heads_copy(source, slot):
        return across(source.at[:, :, :, pl.ds(0, 128)], heads, slot)

    def wait_heads(source, slot):
        @pl.when(section == 0)
        def _():
            heads_copy(source, slot).wait_recv()

        @pl.when(section == 1)
        def _():
            heads_copy(source, slot).wait_send()

    fetch(frames, 0).start()
    fetch(frames, 1).start()
    for layer in range(2):
        start_local_w(layer, w_plan(layer), slot_of[layer])

    barrier = pltpu.get_barrier_semaphore()
    greeted = [dict(sibling)]
    greeted += [at_plane(lax.rem(mp + k, np_)) for k in range(1, np_)]
    greeted += [at_z(lax.rem(mz + k, nz)) for k in range(1, nz)]
    greeted += [dict(axis["partner"], section=other) for axis in bits]
    for where in greeted:
        pl.semaphore_signal(barrier, inc=1, device_id=where, device_id_type=MESH)

    for k, (x, fill) in enumerate(((gains, 0.0), (shifts, -1e30), (recurs, 0.0))):
        vecs[section, k : k + 1, 0:width] = x[...]
        vecs[section, k : k + 1, width:] = jnp.full((1, 2 * W - width), fill, F32)
    vecs[section, 3:8, :] = jnp.zeros((5, 2 * W), F32)

    gap = jnp.zeros((W - rest, W), BF16)

    @pl.when(section == 0)
    def _():
        wc[0, 1, rest:, :] = gap
        wc[1, 1, rest:, :] = gap

    @pl.when(section == 1)
    def _():
        wc[0, 0, rest:, :] = gap
        wc[1, 0, rest:, :] = gap
        wr1[rest:, :] = gap

    for spot in (0, 2):
        tails[spot, rest:, :] = jnp.zeros((W - rest, rest - full), BF16)
    for spare in (f_own, p_own, g3.at[0], g3.at[1]):
        spare[sent_rows:, :] = jnp.zeros((spare.shape[0] - sent_rows, W), BF16)

    pl.semaphore_wait(barrier, len(greeted))

    @pl.when(section == 1)
    def _():
        heads_copy(frames, 1).start()

    for layer in range(2):
        start_across_w(layer, w_plan(layer), slot_of[layer])
    send_vec = across(vecs.at[section], vecs.at[section], 3)
    send_vec.start()

    def stage_copy(where, rnd, slot, k, back):
        buf, parity, size, me, at, send, recv = where
        there = at(lax.rem(me + (size - k if back else k), size))
        ref = buf.at[parity, slot]
        return pltpu.make_async_remote_copy(
            src_ref=ref, dst_ref=ref, send_sem=send.at[rnd, k], recv_sem=recv.at[rnd, k],
            device_id=there, device_id_type=MESH,
        )

    def in_plane(buf, parity):
        return (buf, parity, np_, mp, at_plane, pl_send, pl_recv)

    def in_line(buf, parity):
        return (buf, parity, nz, mz, at_z, z_send, z_recv)

    def stage_start(where, rnd, value):
        buf, parity, size, me = where[:4]
        buf[parity, me] = value
        for k in range(1, size):
            stage_copy(where, rnd, me, k, False).start()

    def stage_wait(where, rnd):
        size, me = where[2:4]
        for k in range(1, size):
            stage_copy(where, rnd, me, k, False).wait_send()
            stage_copy(where, rnd, lax.rem(me + size - k, size), k, True).wait_recv()

    def add_slots(where):
        buf, parity, size = where[:3]
        total = buf[parity, 0]
        for k in range(1, size):
            total = total + buf[parity, k]
        return total

    groups = lengths.shape[1]
    s_at = lax.broadcasted_iota(jnp.int32, (seqs, groups), 0)
    g_at = lax.broadcasted_iota(jnp.int32, (seqs, groups), 1) * views
    there = (s_at >= g_at) & (s_at < g_at + views)
    position = lax.broadcasted_iota(jnp.int32, (seqs, 128), 1)
    local_counts = []
    for m in range(2):
        turn[...] = jnp.zeros_like(turn)
        turn[0:steps, 0:seqs] = masks[m].astype(F32)
        mask = turn[...].T[0:seqs]
        length = jnp.broadcast_to(lengths[m : m + 1, :], (seqs, groups)).astype(F32)
        limit = jnp.sum(jnp.where(there, length, 0.0), axis=1, keepdims=True)
        alive = (position.astype(F32) < limit) & ((mask > 0.0) | (position == 0))
        alive = jnp.where(position < steps, alive.astype(F32), 0.0)
        total = jnp.zeros((seqs, 128), F32)
        for t in range(steps):
            at = m * span + t * seqs
            cells = jnp.broadcast_to(alive[:, t : t + 1], (seqs, 128))
            live[at : at + seqs, :] = cells
            total = total + cells
        local_counts.append(jnp.sum(total, axis=0, keepdims=True))
    n_own = jnp.concatenate(local_counts * 4, axis=0)

    cnt_plane, cnt_line = in_plane(cnt_p, 0), in_line(cnt_z, 0)
    stage_start(cnt_plane, 0, n_own)

    def vec_of(layer, k):
        return vecs[layer, k : k + 1, pl.ds(aligned(section * W, W), W)]

    def matmul_to(out, a, w, first, m):
        r = pl.ds(m * span, span)

        def body(i, _):
            c = pl.ds(aligned(i * HALF, HALF), HALF)
            y = dot(a[r, :], w[:, c], ((1,), (0,)))
            out[r, c] = y if first else out[r, c] + y
            return 0

        lax.fori_loop(0, 2, body, 0)

    def packed(x, y):
        return jnp.concatenate([z[:, k * QUART : (k + 1) * QUART] for z in (x, y) for k in range(4)], axis=0)

    def unpacked(x):
        return jnp.concatenate([x[k : k + 1] for k in range(4)], axis=1)

    def merge_slots(where, counts_of):
        buf, parity, size = where[:3]
        s = [buf[parity, k, 0:4, :] for k in range(size)]
        q = [buf[parity, k, 4:8, :] for k in range(size)]
        n = [wide(counts_of(k), 2) for k in range(size)]
        total, squares, count = sum(s[1:], s[0]), sum(q[1:], q[0]), sum(n[1:], n[0])
        mean = total / count
        for k in range(size):
            d = s[k] / n[k] - mean
            squares = squares + n[k] * d * d
        return jnp.concatenate([total, squares], axis=0)

    def slim_round(which, m):
        return 1 + 2 * which + m, in_plane(slim_p, 2 * m + which % 2), in_line(slim_z, 2 * m + which % 2)

    def forward_stats(layer, m):
        start = jnp.sum(rows[layer, m * span : m * span + seqs, :], axis=0, keepdims=True) * (1.0 / seqs)

        def body(i, carry):
            s, q = carry
            r = pl.ds(aligned(m * span + i * (2 * seqs), 16), 2 * seqs)
            d = rows[layer, r, :] - start
            kept = wide(live[r, :], 8) * d
            return s + fold(kept), q + fold(kept * d)

        zero = jnp.zeros((8, W), F32)
        s, q = lax.fori_loop(0, pairs, body, (zero, zero))
        s, q = jnp.sum(s, axis=0, keepdims=True), jnp.sum(q, axis=0, keepdims=True)
        n = wide(local_counts[m], 8)
        rnd, plane, _ = slim_round(layer, m)
        stage_start(plane, rnd, packed(s + n * start, jnp.maximum(q - s * s / n, 0.0)))

    def forward_middle(layer, m):
        rnd, plane, line = slim_round(layer, m)
        stage_wait(plane, rnd)
        stage_start(line, rnd, merge_slots(plane, lambda k: cnt_p[0, k, m : m + 1, :]))

    def forward_end(layer, m):
        rnd, _, line = slim_round(layer, m)
        stage_wait(line, rnd)
        value = merge_slots(line, lambda k: cnt_z[0, k, m : m + 1, :])
        count = wide(counts[m : m + 1, :], 8)
        mean = unpacked(value[0:4]) / count
        scale = lax.rsqrt(unpacked(value[4:8]) / count + EPS)
        coef[layer, 2 * m : 2 * m + 1, :] = mean
        coef[layer, 2 * m + 1 : 2 * m + 2, :] = scale
        slope = vec_of(layer, 0) * scale
        coef[layer, 4 + 2 * m : 5 + 2 * m, :] = slope
        coef[layer, 5 + 2 * m : 6 + 2 * m, :] = vec_of(layer, 1) - mean * slope

    def forward_scan(layer, m, passes):
        rec = vec_of(layer, 2)
        slope = coef[layer, 4 + 2 * m : 5 + 2 * m, :]
        shift = coef[layer, 5 + 2 * m : 6 + 2 * m, :]

        def body(i, carry):
            h, level = carry
            r = pl.ds(aligned(m * span + i * (2 * seqs), 16), 2 * seqs)
            x = rows[layer, r, :] * slope + shift
            lv = wide(live[r, :], 8)
            alive = lv > 0.0
            both = []
            for k in range(2):
                part = slice(k * seqs, (k + 1) * seqs)
                z = x[part] + rec * h
                soft = jnp.maximum(z, 0.0) + jnp.log(1.0 + jnp.exp(-jnp.abs(z)))
                h = jnp.where(alive[part], soft, h)
                both.append(h)
            two = jnp.concatenate(both, axis=0)
            hid[layer, r, :] = two
            if passes:
                p_own[r, :] = two.astype(BF16)
                level = level + fold(lv * two)
            return h, level

        _, level = lax.fori_loop(0, pairs, body, (jnp.zeros((seqs, W), F32), jnp.zeros((8, W), F32)))
        if not passes:
            return None
        level = jnp.sum(level, axis=0, keepdims=True)
        levels[1:2, :] = level if m == 0 else levels[1:2, :] + level
        here = pl.ds(m * span, span)
        made = across(p_own.at[here, :], p_far.at[here, :], 18 + m)
        made.start()
        return made

    def backward_scan(layer, m, above, between=lambda: None):
        gain, shift, recur = vec_of(layer, 0), vec_of(layer, 1), vec_of(layer, 2)
        for lq in range(4):
            lanes = slice(lq * QUART, (lq + 1) * QUART)
            gq, sq, rec = gain[:, lanes], shift[:, lanes], recur[:, lanes]
            mean = coef[layer, 2 * m : 2 * m + 1, lanes]
            scale = coef[layer, 2 * m + 1 : 2 * m + 2, lanes]

            def body(i, carry):
                down, s1, s2, rsum, sqh, sqa = carry
                i = pairs - 1 - i
                start = m * span + i * (2 * seqs)
                r = pl.ds(aligned(start, 16), 2 * seqs)
                before = pl.ds(aligned(jnp.maximum(start - seqs, 0), 8), seqs)
                normed = (rows[layer, r, lanes] - mean) * scale
                drive = gq * normed + sq
                h2 = hid[layer, r, lanes]
                hb = jnp.where(i > 0, hid[layer, before, lanes], 0.0)
                lv = wide(live[r, :], 2)
                up = above[r, lanes].astype(F32)
                res = f_own[r, lanes].astype(F32)
                aux = res + h2 if layer == 1 else res
                sqh = sqh + fold(lv * (h2 * h2))
                sqa = sqa + fold(lv * (aux * aux))
                grads = [None, None]
                for k in (1, 0):
                    part = slice(k * seqs, (k + 1) * seqs)
                    prior = h2[0:seqs] if k == 1 else hb
                    slope = 0.5 + 0.5 * jnp.tanh(0.5 * (drive[part] + rec * prior))
                    total = up[part] + down
                    gd = lv[part] * slope * total
                    down = (1.0 - lv[part]) * total + rec * gd
                    grads[k] = gd
                    rsum = rsum + fold(gd * prior)
                gd2 = jnp.concatenate(grads, axis=0)
                hid[layer, r, lanes] = gd2
                return down, s1 + fold(gd2), s2 + fold(gd2 * normed), rsum, sqh, sqa

            z8 = jnp.zeros((8, QUART), F32)
            _, s1, s2, rsum, sqh, sqa = lax.fori_loop(
                0, pairs, body, (jnp.zeros((seqs, QUART), F32), z8, z8, z8, z8, z8)
            )
            for k, x in ((m, s1), (2 + m, s2)):
                tot[layer, k : k + 1, lanes] = jnp.sum(x, axis=0, keepdims=True)
            for k, x in ((4, rsum), (5, sqh), (6, sqa)):
                x = jnp.sum(x, axis=0, keepdims=True)
                tot[layer, k : k + 1, lanes] = x if m == 0 else tot[layer, k : k + 1, lanes] + x
            between()

    def backward_stats(layer, m):
        rnd, plane, _ = slim_round(3 - layer, m)
        stage_start(plane, rnd, packed(tot[layer, m : m + 1, :], tot[layer, 2 + m : 3 + m, :]))

    def backward_middle(layer, m):
        rnd, plane, line = slim_round(3 - layer, m)
        stage_wait(plane, rnd)
        stage_start(line, rnd, add_slots(plane))

    def backward_end(layer, m):
        rnd, _, line = slim_round(3 - layer, m)
        stage_wait(line, rnd)
        value = add_slots(line)
        tot[layer, m : m + 1, :] = unpacked(value[0:4])
        tot[layer, 2 + m : 3 + m, :] = unpacked(value[4:8])

    def grad_rows(layer, m, slot):
        gain = vec_of(layer, 0)
        for lh in range(2):
            lanes = slice(lh * HALF, (lh + 1) * HALF)
            mean = coef[layer, 2 * m : 2 * m + 1, lanes]
            scale = coef[layer, 2 * m + 1 : 2 * m + 2, lanes]
            count = wide(counts[m : m + 1, :], 4)
            first = tot[layer, m : m + 1, lanes] / count
            second = tot[layer, 2 + m : 3 + m, lanes] / count * scale
            k = scale * gain[:, lanes]

            def body(i, acc):
                r = pl.ds(aligned(m * span + i * (2 * seqs), 16), 2 * seqs)
                y = hid[layer, r, lanes] - first - (rows[layer, r, lanes] - mean) * second
                y = wide(live[r, :], 4) * (k * y)
                g3[0, r, lanes] = y.astype(BF16)
                return acc + fold(y)

            acc = lax.fori_loop(0, pairs, body, jnp.zeros((8, HALF), F32))
            acc = jnp.sum(acc, axis=0, keepdims=True)
            if m == 0:
                levels[4:5, lanes] = acc
            else:
                top = lax.broadcasted_iota(jnp.int32, (16, HALF), 0) == 0
                minus = jnp.where(top, -(levels[4:5, lanes] + acc), 0.0)
                g3[0, total_rows:sent_rows, lanes] = minus.astype(BF16)
        here = pl.ds(0, span) if m == 0 else pl.ds(span, span + 16)
        made = across(g3.at[0, here, :], g3.at[1, here, :], slot + m)
        made.start()
        return made

    sums_round = {1: (1, 10), 0: (0, 11)}

    def sums_start(layer):
        parity, rnd = sums_round[layer]
        own_sum = -g3[0, total_rows:sent_rows, :].astype(F32)[0:1]
        far_sum = -g3[1, total_rows:sent_rows, :].astype(F32)[0:1]
        value = jnp.concatenate([own_sum, far_sum, tot[layer, 4:7, :], jnp.zeros((3, W), F32)], axis=0)
        stage_start(in_plane(wide_p, parity), rnd, value)

    def sums_middle(layer):
        parity, rnd = sums_round[layer]
        stage_wait(in_plane(wide_p, parity), rnd)
        stage_start(in_line(wide_z, parity), rnd, add_slots(in_plane(wide_p, parity)))

    def sums_end(layer):
        parity, rnd = sums_round[layer]
        stage_wait(in_line(wide_z, parity), rnd)
        vtot[layer] = add_slots(in_line(wide_z, parity))
        tot[layer, 4:7, :] = vtot[layer, 2:5, :]
        tot[layer, 7:8, :] = wide(counts[0:1, :] + counts[1:2, :], 8)
        env["summed"].add(layer)

        @pl.when(section == layer)
        def _():
            pltpu.make_async_copy(tot.at[layer], v.at[section], v_sems.at[0]).start()

        @pl.when(section != layer)
        def _():
            v_across(layer).start()

    def v_across(layer):
        return pltpu.make_async_remote_copy(
            src_ref=tot.at[layer], dst_ref=v.at[section], send_sem=v_sems.at[1], recv_sem=v_sems.at[2],
            device_id=sibling, device_id_type=MESH,
        )

    def transpose(src, begin=0, end=W // 128):
        def body(j, _):
            c = pl.ds(aligned(j * 128, 128), 128)
            src_t[c, 0:total_rows] = src[0:total_rows, c].T
            return 0

        lax.fori_loop(begin, end, body, 0)

    def transpose_level(src, layer):
        top = lax.broadcasted_iota(jnp.int32, (16, W), 0) == 0
        src[total_rows:sent_rows, :] = jnp.where(top, levels[2 + layer : 3 + layer, :], 0.0).astype(BF16)

        def body(j, _):
            c = pl.ds(aligned(j * 128, 128), 128)
            src_t[c, total_rows:] = src[total_rows:, c].T
            level = src[total_rows:sent_rows, c].astype(F32)[0:1]
            column[layer, c, :] = jnp.broadcast_to(level, (128, 128)).T.astype(BF16)
            return 0

        lax.fori_loop(0, W // 128, body, 0)

    def weight_part(block, grads, c):
        lanes = pl.ds(c * QUART, QUART)

        def body(j, _):
            r = pl.ds(aligned(j * HALF, HALF), HALF)
            block[r, lanes] = dot(src_t[r, :], grads[:, lanes], ((1,), (0,))).astype(BF16)
            return 0

        lax.fori_loop(0, W // HALF, body, 0)

    def source_grad(store, w_own, w_far, between):
        for m in range(2):
            r = pl.ds(m * span, span)

            def body(i, _):
                c = pl.ds(aligned(i * HALF, HALF), HALF)
                y = dot(g3[0, r, :], w_own[c, :], ((1,), (1,))) + dot(g3[1, r, :], w_far[c, :], ((1,), (1,)))
                store(r, c, y)
                return 0

            lax.fori_loop(0, 2, body, 0)
            between()

    env = dict(summed=set(), vtot=vtot, column=column, space=space, ar_send=ar_send, ar_recv=ar_recv,
               ar_other=ar_other, o=o, section=section, here={"batch": b})
    xs = [a for a in bits if a["link"] == "x"]
    ys = [a for a in bits if a["link"] == "y"]
    zs = [a for a in bits if a["link"] == "z"]
    orders = (xs + ys + zs, ys + xs + zs)
    blocks = {
        (1, 0): f_far.at[pl.ds(0, W), :],
        (1, 1): p_far.at[pl.ds(0, W), :],
        (0, 0): wc.at[1, 1],
        (0, 1): wr1,
    }
    parts = {}
    for layer in (1, 0):
        for index in range(4):
            part, side = index // 2, index % 2

            def lane_of(sec, part=part, side=side):
                return (sec if part == 0 else 1 - sec) * W + side * HALF

            block = blocks[layer, part].at[:, pl.ds(side * HALF, HALF)]
            parts[layer, index] = Reduction(env, layer, index, block, orders, lane_of)
    order = Order()

    def weight_grads(layer, between):
        for part in range(2):
            if part == 1:
                between()
            for c in range(4):
                weight_part(blocks[layer, part], g3.at[part], c)
                order.work(0.9)
                order.begin(parts[layer, 2 * part + c // 2], c % 2)

    def arrived(layer, sends):
        for made in sends:
            made.wait()
        sums_start(layer)

    wait_heads(frames, 1)
    send_f = []
    for m in range(2):
        by_units(frames, f_own, m)
        fetch(grad_out, m).start()
        here = pl.ds(m * span, span)
        made = across(f_own.at[here, :], f_far.at[here, :], (0, 24)[m])
        made.start()
        send_f.append(made)

    stage_wait(cnt_plane, 0)
    stage_start(cnt_line, 0, add_slots(cnt_plane))
    wait_w(0, w_plan(0), slot_of[0], 0)
    matmul_to(rows.at[0], f_own, wc.at[0, 0], True, 0)
    wait_w(0, w_plan(0), slot_of[0], 1)
    send_f[0].wait()
    matmul_to(rows.at[0], f_far, wc.at[0, 1], False, 0)
    forward_stats(0, 0)
    matmul_to(rows.at[0], f_own, wc.at[0, 0], True, 1)
    forward_middle(0, 0)
    send_f[1].wait()

    @pl.when(section == 1)
    def _():
        heads_copy(grad_out, 2).start()

    matmul_to(rows.at[0], f_far, wc.at[0, 1], False, 1)
    forward_stats(0, 1)
    send_vec.wait_send()
    across(vecs.at[other], vecs.at[other], 3).wait_recv()
    stage_wait(cnt_line, 0)
    counts[...] = add_slots(cnt_line)
    forward_end(0, 0)
    sends = [forward_scan(0, 0, True)]
    forward_middle(0, 1)
    wait_heads(grad_out, 2)
    by_units(grad_out, g3.at[1], 0)
    forward_end(0, 1)
    sends.append(forward_scan(0, 1, True))
    wait_w(1, w_plan(1), slot_of[1], 0)
    matmul_to(rows.at[1], p_own, wc.at[1, 0], True, 0)
    wait_w(1, w_plan(1), slot_of[1], 1)
    sends[0].wait()
    matmul_to(rows.at[1], p_far, wc.at[1, 1], False, 0)
    forward_stats(1, 0)
    matmul_to(rows.at[1], p_own, wc.at[1, 0], True, 1)
    forward_middle(1, 0)
    sends[1].wait()
    matmul_to(rows.at[1], p_far, wc.at[1, 1], False, 1)
    forward_stats(1, 1)
    done_w(0, w_plan(0), slot_of[0])

    start_local_w(0, late_plan, slot_of[2])
    start_across_w(0, late_plan, slot_of[2])

    @pl.when(section == 1)
    def _():
        wc[0, 1, width - late_row :, :] = jnp.zeros((W - width + late_row, W), BF16)

    def source_level():
        def body(i, acc):
            r = pl.ds(aligned(i * (2 * seqs), 16), 2 * seqs)
            return acc + fold(wide(live[r, :], 8) * f_own[r, :].astype(F32))

        acc = lax.fori_loop(0, 2 * pairs, body, jnp.zeros((8, W), F32))
        levels[0:1, :] = jnp.sum(acc, axis=0, keepdims=True)

    forward_end(1, 0)
    forward_scan(1, 0, False)
    forward_middle(1, 1)
    by_units(grad_out, g3.at[1], 1)
    source_level()
    forward_end(1, 1)
    level_plane, level_line = in_plane(wide_p, 0), in_line(wide_z, 0)
    stage_start(level_plane, 9, jnp.concatenate([levels[0:2, :], jnp.zeros((6, W), F32)], axis=0))
    forward_scan(1, 1, False)
    backward_scan(1, 0, g3.at[1])
    backward_stats(1, 0)
    stage_wait(level_plane, 9)
    stage_start(level_line, 9, add_slots(level_plane))
    backward_scan(1, 1, g3.at[1])
    backward_stats(1, 1)
    backward_middle(1, 0)
    pl.semaphore_signal(credit.at[0], inc=1, device_id=sibling, device_id_type=MESH)
    transpose(p_own, 0, W // 256)
    backward_middle(1, 1)
    backward_end(1, 0)
    pl.semaphore_wait(credit.at[0], 1)
    sends = [grad_rows(1, 0, 20)]
    transpose(p_own, W // 256)
    stage_wait(level_line, 9)
    levels[2:4, :] = (add_slots(level_line) / wide(counts[0:1, :] + counts[1:2, :], 8))[0:2]
    transpose_level(p_own, 1)
    backward_end(1, 1)
    sends.append(grad_rows(1, 1, 20))
    weight_grads(1, lambda: arrived(1, sends))
    wait_w(1, w_plan(1), slot_of[1], 2)
    done_w(1, w_plan(1), slot_of[1])

    def keep_down(r, c, y):
        p_own[r, c] = y.astype(BF16)

    source_grad(keep_down, wc.at[1, 0], wr1, lambda: order.work(3.0))
    pl.semaphore_signal(credit.at[1], inc=1, device_id=sibling, device_id_type=MESH)
    sums_middle(1)
    backward_scan(0, 0, p_own, lambda: order.work(0.6))
    backward_stats(0, 0)
    backward_scan(0, 1, p_own, lambda: order.work(0.6))
    backward_stats(0, 1)
    backward_middle(0, 0)
    sums_end(1)
    transpose(f_own)
    transpose_level(f_own, 0)
    backward_middle(0, 1)
    order.work(3.0)
    backward_end(0, 0)
    pl.semaphore_wait(credit.at[1], 1)
    sends = [grad_rows(0, 0, 22)]
    backward_end(0, 1)
    sends.append(grad_rows(0, 1, 22))
    order.work(2.0)
    weight_grads(0, lambda: arrived(0, sends))
    wait_w(0, late_plan, slot_of[2], 0)
    wait_w(0, late_plan, slot_of[2], 1)
    done_w(0, late_plan, slot_of[2])

    def keep_source(r, c, y):
        rows[0, r, c] = y

    fetch(grad_out, 0).start()
    fetch(grad_out, 1).start()
    sums_middle(0)
    source_grad(keep_source, wc.at[0, 0], wc.at[0, 1], lambda: order.work(3.0))
    sums_end(0)

    def give(m):
        return pltpu.make_async_copy(staged.at[m], gf.at[m], stage_sem.at[m])

    for m in range(2):
        fetch(grad_out, m).wait()

        def finish_frames(i, _, m=m):
            straight = staged[m, pl.ds(2 * i, 2)].astype(F32).reshape(2 * seqs, half)
            y = rows[0, pl.ds(aligned(m * span + 2 * i * seqs, 8), 2 * seqs), :]
            y = jnp.where(section == 0, y[:, :half], y[:, late_shift : late_shift + half])
            staged[m, pl.ds(2 * i, 2)] = (y + straight).reshape(2, seqs, half).astype(BF16)
            return 0

        lax.fori_loop(0, pairs, finish_frames, 0)
        give(m).start()
        order.work(2.0)
    order.drain()
    for m in range(2):
        give(m).wait()

    for layer in range(2):

        @pl.when(section == layer)
        def _(layer=layer):
            pltpu.make_async_copy(tot.at[layer], v.at[section], v_sems.at[0]).wait()
            pltpu.make_async_remote_copy(
                src_ref=tot.at[layer], dst_ref=v.at[other], send_sem=v_sems.at[1], recv_sem=v_sems.at[2],
                device_id=sibling, device_id_type=MESH,
            ).wait_recv()

        @pl.when(section != layer)
        def _(layer=layer):
            v_across(layer).wait_send()

    own_part, far_part = v[section], v[other]
    first = jnp.where(section == 0, own_part, far_part)
    second = jnp.where(section == 0, far_part, own_part)
    for row, terms in ((0, (2, 3)), (1, (0, 1)), (2, (4,))):
        for lane, x in ((0, first), (W, second)):
            total = x[terms[0] : terms[0] + 1, :]
            for k in terms[1:]:
                total = total + x[k : k + 1, :]
            vectors[row : row + 1, lane : lane + W] = total
    squares = jnp.sum(first[5:7, :] + second[5:7, :], axis=1, keepdims=True)
    root = jnp.sqrt(squares / (first[7:8, 0:1] * width))
    for k in range(2):
        vectors[3 + k : 4 + k, :] = jnp.broadcast_to(root[k : k + 1], (1, 2 * W))
    vectors[5:8, :] = jnp.zeros((3, 2 * W), F32)


def write_results(o, gf, vectors, grad_weight, grad_frames, grad_gains, grad_shifts, grad_recurs, table):
    width = grad_weight.shape[2]
    grad_weight[0] = o[...][:, :width].astype(F32)
    grad_frames[...] = gf[...]

    @pl.when(pl.program_id(0) == 0)
    def _():
        for k, out in enumerate((grad_gains, grad_shifts, grad_recurs)):
            out[...] = vectors[k : k + 1, 0:width]
        table[...] = jnp.concatenate([vectors[3:4, 0:1], vectors[4:5, 0:1]], axis=1)


def results(o, gf, vectors):
    micro, steps, seqs, half = gf.shape
    width = 2 * half
    count = W * 2 // 256
    frames = micro * steps // count
    whole = lambda shape: pl.BlockSpec(shape, lambda i: (0, 0))
    out = pl.pallas_call(
        write_results,
        grid=(count,),
        in_specs=[
            pl.BlockSpec((256, 2 * W), lambda i: (i, 0)),
            pl.BlockSpec((frames, seqs, half), lambda i: (i, 0, 0)),
            whole((8, 2 * W)),
        ],
        out_specs=(
            pl.BlockSpec((1, 256, width), lambda i: (0, i, 0)),
            pl.BlockSpec((frames, seqs, half), lambda i: (i, 0, 0)),
            whole((1, width)),
            whole((1, width)),
            whole((1, width)),
            whole((1, 2)),
        ),
        out_shape=(
            jax.ShapeDtypeStruct((1, width, width), F32),
            jax.ShapeDtypeStruct((micro * steps, seqs, half), BF16),
            jax.ShapeDtypeStruct((1, width), F32),
            jax.ShapeDtypeStruct((1, width), F32),
            jax.ShapeDtypeStruct((1, width), F32),
            jax.ShapeDtypeStruct((1, 2), F32),
        ),
        compiler_params=pltpu.CompilerParams(vmem_limit_bytes=64 * 1024 * 1024),
    )(o.reshape(2 * W, 2 * W), gf.reshape(micro * steps, seqs, half), vectors)
    return out[1].reshape(gf.shape), out[0], *out[2:]


def whole_step(dims, frames, grad_out, weights, gains, shifts, recurs, lengths, masks):
    nz, ny, nx = dims
    micro, steps, seqs, half = frames.shape
    width = 2 * half
    views = seqs // lengths.shape[1]
    rows = micro * steps * seqs
    np_ = ny * nx
    wide_rows = (rows + 16 + 127) // 128 * 128
    depth = (nx * ny * nz - 1).bit_length()
    any_ = pl.BlockSpec(memory_space=pl.ANY)
    held = pl.BlockSpec(memory_space=pltpu.VMEM)
    dma = pltpu.SemaphoreType.DMA
    return pl.pallas_call(
        functools.partial(kernel, dims, steps, seqs, views),
        out_shape=(
            jax.ShapeDtypeStruct((2, W, 2 * W), BF16),
            jax.ShapeDtypeStruct(frames.shape, BF16),
            jax.ShapeDtypeStruct((8, 2 * W), F32),
        ),
        in_specs=[any_] * 3 + [held] * 5,
        out_specs=(any_, any_, held),
        scratch_shapes=[
            pltpu.VMEM((wide_rows, W), BF16),
            pltpu.VMEM((rows, W), BF16),
            pltpu.VMEM((wide_rows, W), BF16),
            pltpu.VMEM((rows, W), BF16),
            pltpu.VMEM((2, wide_rows, W), BF16),
            pltpu.VMEM((2, 2, W, W), BF16),
            pltpu.VMEM((W, W), BF16),
            pltpu.VMEM((W, wide_rows), BF16),
            pltpu.VMEM((rows, 128), F32),
            pltpu.VMEM((128, 128), F32),
            pltpu.VMEM(frames.shape, BF16),
            pltpu.VMEM((micro, steps, seqs, 128), BF16),
            pltpu.VMEM((5, W, (width - W) % 128), BF16),
            pltpu.VMEM((2, 8, W), F32),
            pltpu.VMEM((2, 8, 2 * W), F32),
            pltpu.VMEM((2, rows, W), F32),
            pltpu.VMEM((2, rows, W), F32),
            pltpu.VMEM((2, 8, W), F32),
            pltpu.VMEM((2, 8, W), F32),
            pltpu.VMEM((2, 8, W), F32),
            pltpu.VMEM((8, W), F32),
            pltpu.VMEM((2, W, 128), BF16),
            pltpu.VMEM((8, 128), F32),
            pltpu.VMEM((1, np_, 8, 128), F32),
            pltpu.VMEM((1, nz, 8, 128), F32),
            pltpu.VMEM((4, np_, 8, QUART), F32),
            pltpu.VMEM((4, nz, 8, QUART), F32),
            pltpu.VMEM((2, np_, 8, W), F32),
            pltpu.VMEM((2, nz, 8, W), F32),
            pltpu.VMEM((2, 4, W, HALF), BF16),
            dma((3, 25)),
            dma((3,)),
            dma((2,)),
            pltpu.SemaphoreType.REGULAR((2,)),
            dma((12, max(np_, 2))),
            dma((12, max(np_, 2))),
            dma((12, max(nz, 2))),
            dma((12, max(nz, 2))),
            dma((2, 4, 2, 2 * depth + 2)),
            dma((2, 4, 2, 2 * depth + 2)),
            dma((2, 4, 2, 2)),
        ],
        compiler_params=pltpu.CompilerParams(
            collective_id=0, has_side_effects=True, vmem_limit_bytes=64 * 1024 * 1024
        ),
    )(frames, grad_out, weights, gains, shifts, recurs, lengths, masks)


def shards(dims, frames, grad_out, weights, gains, shifts, recurs, lengths, masks):
    return results(*whole_step(dims, frames, grad_out, weights, gains, shifts, recurs, lengths, masks))


def solution(mesh):
    in_specs = (
        P(None, None, "batch", "section"),
        P(None, None, "batch", "section"),
        P("section", None, None),
        P("section", None),
        P("section", None),
        P("section", None),
        P(None, "batch"),
        P(None, None, "batch"),
    )
    out_specs = (
        P(None, None, "batch", "section"),
        P("section", None, None),
        P("section", None),
        P("section", None),
        P("section", None),
        P("section", None),
    )
    body = functools.partial(shards, grid_of(mesh.shape["batch"]))
    return jax.shard_map(body, mesh=mesh, in_specs=in_specs, out_specs=out_specs, check_vma=False)
```

profile of v0, /device:TPU:0, one launch (start us, length us, event | category | flops | bytes accessed | tf_op | source)
XLA Modules:
  0.0 223.3 jit_solution(1803843796623389671)
XLA Ops:
  0.6 210.9 %shard_map.127 = (bf16[2,1024,2048]{2,1,0:T(8,128)(2,1)}, bf16[2,24,24,1000]{3,2,1,0:T(8,128)(2,1)}, f32[8,2048]{1,0:T(8,128)}) custom-call(bf16[2,24,24,1000]{3,2,1,0:T(8,128)(2,1)} %frames.1, bf16[2,24,24,1000]{3,2,1,0:T(8,128)(2,1)} %grad_out.1, bf16[1,2000,2000]{2,1,0:T(8,128)(2,1)} %weights.1, f32[1,2000]{1,0:T(1,128)} %gains.1, f32[1,2000]{1,0:T(1,128)} %shifts.1, ...), custom_call_target="tpu_custom_call" | custom-call | tf_op jit(solution)/shard_map/pallas_call | solution.py:1140
  211.5 11.6 %shard_map.128 = (f32[1,2000,2000]{2,1,0:T(8,128)}, bf16[48,24,1000]{2,1,0:T(8,128)(2,1)}, f32[1,2000]{1,0:T(1,128)}, f32[1,2000]{1,0:T(1,128)}, f32[1,2000]{1,0:T(1,128)}, /*index=5*/f32[1,2]{1,0:T(1,128)}) custom-call(bf16[2048,2048]{1,0:T(8,128)(2,1)} %bitcast.3, bf16[48,24,1000]{2,1,0:T(8,128)(2,1)} %bitcast.4, f32[8,2048]{1,0:T(8,128)} %get-tuple-element.17.vectors), custom_call_target="tpu_custom_call" | custom-call | tf_op jit(solution)/shard_map/pallas_call | solution.py:1099
where the time goes:
time: 224 us; the launch traced here: 223 us
  Pallas kernels  222 us (99%)
    pallas_call x1, Pallas kernels, whole_step(): pl.pallas_call(functools.partial(kernel, dims, steps, seqs, views), out_s...  211 us
    pallas_call x1, Pallas kernels, results(): pl.pallas_call(write_results, grid=(count,), in_specs=[pl.BlockSpec((256,...  11.6 us

commit v1 on v0

--- a/solution.py
+++ b/solution.py
@@ -253,7 +253,7 @@
 
 
 class Order:
-    RATE, HOP = 50e3, 1.8
+    RATE, HOP = 70e3, 1.8
 
     def __init__(self):
         self.now = 0.0
@@ -348,11 +348,12 @@
 
         @pl.when(section == 0)
         def _():
+            pad = jnp.zeros((2 * seqs, lead), F32)
+
             def place(i, _):
                 x = staged[m, pl.ds(2 * i, 2)].astype(F32).reshape(2 * seqs, half)
-                head = heads[m, pl.ds(2 * i, 2)].astype(F32).reshape(2 * seqs, 128)
                 to = pl.ds(aligned(m * span + 2 * i * seqs, 16), 2 * seqs)
-                target[to, :] = jnp.concatenate([x, head[:, :lead]], axis=1).astype(BF16)
+                target[to, :] = jnp.concatenate([x, pad], axis=1).astype(BF16)
                 return 0
 
             lax.fori_loop(0, pairs, place, 0)
@@ -365,6 +366,21 @@
                 x = staged[m, pl.ds(2 * i, 2)].astype(F32).reshape(2 * seqs, half)
                 to = pl.ds(aligned(m * span + 2 * i * seqs, 16), 2 * seqs)
                 target[to, :] = jnp.concatenate([x[:, lead:], pad], axis=1).astype(BF16)
+                return 0
+
+            lax.fori_loop(0, pairs, place, 0)
+
+    def patch_heads(target, m):
+        @pl.when(section == 0)
+        def _():
+            lane = lax.broadcasted_iota(jnp.int32, (2 * seqs, 128), 1)
+
+            def place(i, _):
+                to = pl.ds(aligned(m * span + 2 * i * seqs, 16), 2 * seqs)
+                head = heads[m, pl.ds(2 * i, 2)].astype(F32).reshape(2 * seqs, 128)
+                head = pltpu.roll(head, 128 - lead, 1)
+                old = target[to, W - 128 :].astype(F32)
+                target[to, W - 128 :] = jnp.where(lane < 128 - lead, old, head).astype(BF16)
                 return 0
 
             lax.fori_loop(0, pairs, place, 0)
@@ -509,8 +525,7 @@
     def _():
         heads_copy(frames, 1).start()
 
-    for layer in range(2):
-        start_across_w(layer, w_plan(layer), slot_of[layer])
+    start_across_w(0, w_plan(0), slot_of[0])
     send_vec = across(vecs.at[section], vecs.at[section], 3)
     send_vec.start()
 
@@ -833,7 +848,7 @@
         lax.fori_loop(0, W // 128, body, 0)
 
     def weight_part(block, grads, c):
-        lanes = pl.ds(c * QUART, QUART)
+        lanes = pl.ds(c * HALF, HALF)
 
         def body(j, _):
             r = pl.ds(aligned(j * HALF, HALF), HALF)
@@ -883,36 +898,38 @@
         for part in range(2):
             if part == 1:
                 between()
-            for c in range(4):
+            for c in range(2):
                 weight_part(blocks[layer, part], g3.at[part], c)
-                order.work(0.9)
-                order.begin(parts[layer, 2 * part + c // 2], c % 2)
+                order.work(2.0)
+                order.begin(parts[layer, 2 * part + c], 0)
+                order.begin(parts[layer, 2 * part + c], 1)
 
     def arrived(layer, sends):
         for made in sends:
             made.wait()
         sums_start(layer)
 
-    wait_heads(frames, 1)
     send_f = []
     for m in range(2):
         by_units(frames, f_own, m)
         fetch(grad_out, m).start()
+        if m == 0:
+            wait_heads(frames, 1)
+        patch_heads(f_own, m)
         here = pl.ds(m * span, span)
         made = across(f_own.at[here, :], f_far.at[here, :], (0, 24)[m])
         made.start()
         send_f.append(made)
-
+    start_across_w(1, w_plan(1), slot_of[1])
     stage_wait(cnt_plane, 0)
     stage_start(cnt_line, 0, add_slots(cnt_plane))
     wait_w(0, w_plan(0), slot_of[0], 0)
     matmul_to(rows.at[0], f_own, wc.at[0, 0], True, 0)
+    matmul_to(rows.at[0], f_own, wc.at[0, 0], True, 1)
     wait_w(0, w_plan(0), slot_of[0], 1)
     send_f[0].wait()
     matmul_to(rows.at[0], f_far, wc.at[0, 1], False, 0)
     forward_stats(0, 0)
-    matmul_to(rows.at[0], f_own, wc.at[0, 0], True, 1)
-    forward_middle(0, 0)
     send_f[1].wait()
 
     @pl.when(section == 1)
@@ -920,6 +937,7 @@
         heads_copy(grad_out, 2).start()
 
     matmul_to(rows.at[0], f_far, wc.at[0, 1], False, 1)
+    forward_middle(0, 0)
     forward_stats(0, 1)
     send_vec.wait_send()
     across(vecs.at[other], vecs.at[other], 3).wait_recv()
@@ -928,8 +946,9 @@
     forward_end(0, 0)
     sends = [forward_scan(0, 0, True)]
     forward_middle(0, 1)
+    by_units(grad_out, g3.at[1], 0)
     wait_heads(grad_out, 2)
-    by_units(grad_out, g3.at[1], 0)
+    patch_heads(g3.at[1], 0)
     forward_end(0, 1)
     sends.append(forward_scan(0, 1, True))
     wait_w(1, w_plan(1), slot_of[1], 0)
@@ -964,6 +983,7 @@
     forward_scan(1, 0, False)
     forward_middle(1, 1)
     by_units(grad_out, g3.at[1], 1)
+    patch_heads(g3.at[1], 1)
     source_level()
     forward_end(1, 1)
     level_plane, level_line = in_plane(wide_p, 0), in_line(wide_z, 0)

time: 224 us -> 223 us (level)
  no operation moved by 1% of the time
where the time goes in v1:
time: 223 us
  Pallas kernels  222 us (100%)
    pallas_call x1, Pallas kernels, whole_step(): pl.pallas_call(functools.partial(kernel, dims, steps, seqs, views), out_s...  210 us
    pallas_call x1, Pallas kernels, results(): pl.pallas_call(write_results, grid=(count,), in_specs=[pl.BlockSpec((256,...  11.6 us

profile of v1, /device:TPU:0, one launch (start us, length us, event | category | flops | bytes accessed | tf_op | source)
XLA Modules:
  0.0 222.8 jit_solution(14691727639779349436)
XLA Ops:
  0.6 210.4 %shard_map.127 = (bf16[2,1024,2048]{2,1,0:T(8,128)(2,1)}, bf16[2,24,24,1000]{3,2,1,0:T(8,128)(2,1)}, f32[8,2048]{1,0:T(8,128)}) custom-call(bf16[2,24,24,1000]{3,2,1,0:T(8,128)(2,1)} %frames.1, bf16[2,24,24,1000]{3,2,1,0:T(8,128)(2,1)} %grad_out.1, bf16[1,2000,2000]{2,1,0:T(8,128)(2,1)} %weights.1, f32[1,2000]{1,0:T(1,128)} %gains.1, f32[1,2000]{1,0:T(1,128)} %shifts.1, ...), custom_call_target="tpu_custom_call" | custom-call | tf_op jit(solution)/shard_map/pallas_call | solution.py:1160
  211.0 11.6 %shard_map.128 = (f32[1,2000,2000]{2,1,0:T(8,128)}, bf16[48,24,1000]{2,1,0:T(8,128)(2,1)}, f32[1,2000]{1,0:T(1,128)}, f32[1,2000]{1,0:T(1,128)}, f32[1,2000]{1,0:T(1,128)}, /*index=5*/f32[1,2]{1,0:T(1,128)}) custom-call(bf16[2048,2048]{1,0:T(8,128)(2,1)} %bitcast.3, bf16[48,24,1000]{2,1,0:T(8,128)(2,1)} %bitcast.4, f32[8,2048]{1,0:T(8,128)} %get-tuple-element.17.vectors), custom_call_target="tpu_custom_call" | custom-call | tf_op jit(solution)/shard_map/pallas_call | solution.py:1119

commit v2 on v1

--- a/solution.py
+++ b/solution.py
@@ -11,6 +11,8 @@
 W = 1024
 HALF = W // 2
 QUART = W // 4
+PAIRS = 1
+PART = W // PAIRS // 2
 MESH = pl.DeviceIdType.MESH
 F32 = jnp.float32
 BF16 = jnp.bfloat16
@@ -60,7 +62,7 @@
         self.steps += [self.give, self.finish]
 
     def halves(self, i, order):
-        row, rows, lane, lanes = 0, W, i * QUART, QUART
+        row, rows, lane, lanes = 0, W, i * PART, PART
         out = [(row, rows, lane, lanes)]
         for axis in order:
             if rows > 16:
@@ -102,7 +104,7 @@
     def came_at(self, i, k):
         row = sum(r[1] for r in self.regions[i][1 : k + 1])
         _, rows, _, lanes = self.regions[i][k + 1]
-        return row, rows, i * QUART, lanes
+        return row, rows, i * PART, lanes
 
     def scatter(self, k):
         if k > 0:
@@ -141,8 +143,8 @@
             lane = aligned(lane, 128)
             extra = None
             if last:
-                part = self.index // 2
-                first = aligned((self.index % 2) * HALF + lane, 128)
+                part = self.index // PAIRS
+                first = aligned((self.index % PAIRS) * 2 * PART + lane, 128)
                 extra = self.env["vtot"][self.layer, part : part + 1, pl.ds(first, lanes)]
             out.append((row, lane, lanes, at, at_lane, self.local(i, k + 1)[0], extra))
 
@@ -189,11 +191,11 @@
 
     def result(self, i, bit, section):
         rows = self.regions[i][1][1]
-        lane = aligned(self.lane_of(section) + i * QUART, QUART)
-        return self.env["o"].at[section, pl.ds(aligned(bit * rows, 16), rows), pl.ds(lane, QUART)]
+        lane = aligned(self.lane_of(section) + i * PART, PART)
+        return self.env["o"].at[section, pl.ds(aligned(bit * rows, 16), rows), pl.ds(lane, PART)]
 
     def gathered(self, i):
-        return self.space.at[pl.ds(0, self.regions[i][1][1]), pl.ds(i * QUART, QUART)]
+        return self.space.at[pl.ds(0, self.regions[i][1][1]), pl.ds(i * PART, PART)]
 
     def deliver(self, i, near, straight):
         axis, section = self.orders[i][0], self.env["section"]
@@ -233,7 +235,7 @@
                 self.deliver(i, True, False).start()
 
         for i, order in enumerate(self.orders):
-            self.sent.append((order[0]["link"], self.regions[i][1][1] * QUART * 2))
+            self.sent.append((order[0]["link"], self.regions[i][1][1] * PART * 2))
 
     def finish(self):
         @pl.when(self.env["section"] == self.layer)
@@ -884,13 +886,13 @@
     }
     parts = {}
     for layer in (1, 0):
-        for index in range(4):
-            part, side = index // 2, index % 2
+        for index in range(2 * PAIRS):
+            part, side = index // PAIRS, index % PAIRS
 
             def lane_of(sec, part=part, side=side):
-                return (sec if part == 0 else 1 - sec) * W + side * HALF
-
-            block = blocks[layer, part].at[:, pl.ds(side * HALF, HALF)]
+                return (sec if part == 0 else 1 - sec) * W + side * 2 * PART
+
+            block = blocks[layer, part].at[:, pl.ds(side * 2 * PART, 2 * PART)]
             parts[layer, index] = Reduction(env, layer, index, block, orders, lane_of)
     order = Order()
 
@@ -901,8 +903,8 @@
             for c in range(2):
                 weight_part(blocks[layer, part], g3.at[part], c)
                 order.work(2.0)
-                order.begin(parts[layer, 2 * part + c], 0)
-                order.begin(parts[layer, 2 * part + c], 1)
+                for k in range(c * HALF // PART, (c + 1) * HALF // PART):
+                    order.begin(parts[layer, part * PAIRS + k // 2], k % 2)
 
     def arrived(layer, sends):
         for made in sends:
@@ -1196,7 +1198,7 @@
             pltpu.VMEM((4, nz, 8, QUART), F32),
             pltpu.VMEM((2, np_, 8, W), F32),
             pltpu.VMEM((2, nz, 8, W), F32),
-            pltpu.VMEM((2, 4, W, HALF), BF16),
+            pltpu.VMEM((2, 2 * PAIRS, W, 2 * PART), BF16),
             dma((3, 25)),
             dma((3,)),
             dma((2,)),
@@ -1205,9 +1207,9 @@
             dma((12, max(np_, 2))),
             dma((12, max(nz, 2))),
             dma((12, max(nz, 2))),
-            dma((2, 4, 2, 2 * depth + 2)),
-            dma((2, 4, 2, 2 * depth + 2)),
-            dma((2, 4, 2, 2)),
+            dma((2, 2 * PAIRS, 2, 2 * depth + 2)),
+            dma((2, 2 * PAIRS, 2, 2 * depth + 2)),
+            dma((2, 2 * PAIRS, 2, 2)),
         ],
         compiler_params=pltpu.CompilerParams(
             collective_id=0, has_side_effects=True, vmem_limit_bytes=64 * 1024 * 1024

time: 223 us -> 223 us (level)
  no operation moved by 1% of the time
where the time goes in v2:
time: 223 us
  Pallas kernels  222 us (100%)
    pallas_call x1, Pallas kernels, whole_step(): pl.pallas_call(functools.partial(kernel, dims, steps, seqs, views), out_s...  210 us
    pallas_call x1, Pallas kernels, results(): pl.pallas_call(write_results, grid=(count,), in_specs=[pl.BlockSpec((256,...  11.6 us

profile of v2, /device:TPU:0, one launch (start us, length us, event | category | flops | bytes accessed | tf_op | source)
XLA Modules:
  0.0 222.9 jit_solution(1841833183457734727)
XLA Ops:
  0.6 210.5 %shard_map.127 = (bf16[2,1024,2048]{2,1,0:T(8,128)(2,1)}, bf16[2,24,24,1000]{3,2,1,0:T(8,128)(2,1)}, f32[8,2048]{1,0:T(8,128)}) custom-call(bf16[2,24,24,1000]{3,2,1,0:T(8,128)(2,1)} %frames.1, bf16[2,24,24,1000]{3,2,1,0:T(8,128)(2,1)} %grad_out.1, bf16[1,2000,2000]{2,1,0:T(8,128)(2,1)} %weights.1, f32[1,2000]{1,0:T(1,128)} %gains.1, f32[1,2000]{1,0:T(1,128)} %shifts.1, ...), custom_call_target="tpu_custom_call" | custom-call | tf_op jit(solution)/shard_map/pallas_call | solution.py:1162
  211.1 11.6 %shard_map.128 = (f32[1,2000,2000]{2,1,0:T(8,128)}, bf16[48,24,1000]{2,1,0:T(8,128)(2,1)}, f32[1,2000]{1,0:T(1,128)}, f32[1,2000]{1,0:T(1,128)}, f32[1,2000]{1,0:T(1,128)}, /*index=5*/f32[1,2]{1,0:T(1,128)}) custom-call(bf16[2048,2048]{1,0:T(8,128)(2,1)} %bitcast.3, bf16[48,24,1000]{2,1,0:T(8,128)(2,1)} %bitcast.4, f32[8,2048]{1,0:T(8,128)} %get-tuple-element.17.vectors), custom_call_target="tpu_custom_call" | custom-call | tf_op jit(solution)/shard_map/pallas_call | solution.py:1121

commit v3 on v1

--- a/solution.py
+++ b/solution.py
@@ -253,7 +253,7 @@
 
 
 class Order:
-    RATE, HOP = 70e3, 1.8
+    RATE, HOP = 52e3, 2.2
 
     def __init__(self):
         self.now = 0.0
@@ -900,7 +900,7 @@
                 between()
             for c in range(2):
                 weight_part(blocks[layer, part], g3.at[part], c)
-                order.work(2.0)
+                order.work(2.8)
                 order.begin(parts[layer, 2 * part + c], 0)
                 order.begin(parts[layer, 2 * part + c], 1)
 
@@ -1015,25 +1015,25 @@
     def keep_down(r, c, y):
         p_own[r, c] = y.astype(BF16)
 
-    source_grad(keep_down, wc.at[1, 0], wr1, lambda: order.work(3.0))
+    source_grad(keep_down, wc.at[1, 0], wr1, lambda: order.work(4.0))
     pl.semaphore_signal(credit.at[1], inc=1, device_id=sibling, device_id_type=MESH)
     sums_middle(1)
-    backward_scan(0, 0, p_own, lambda: order.work(0.6))
+    backward_scan(0, 0, p_own, lambda: order.work(1.0))
     backward_stats(0, 0)
-    backward_scan(0, 1, p_own, lambda: order.work(0.6))
+    backward_scan(0, 1, p_own, lambda: order.work(1.0))
     backward_stats(0, 1)
     backward_middle(0, 0)
     sums_end(1)
     transpose(f_own)
     transpose_level(f_own, 0)
     backward_middle(0, 1)
-    order.work(3.0)
+    order.work(8.0)
     backward_end(0, 0)
     pl.semaphore_wait(credit.at[1], 1)
     sends = [grad_rows(0, 0, 22)]
     backward_end(0, 1)
     sends.append(grad_rows(0, 1, 22))
-    order.work(2.0)
+    order.work(4.0)
     weight_grads(0, lambda: arrived(0, sends))
     wait_w(0, late_plan, slot_of[2], 0)
     wait_w(0, late_plan, slot_of[2], 1)
@@ -1045,7 +1045,7 @@
     fetch(grad_out, 0).start()
     fetch(grad_out, 1).start()
     sums_middle(0)
-    source_grad(keep_source, wc.at[0, 0], wc.at[0, 1], lambda: order.work(3.0))
+    source_grad(keep_source, wc.at[0, 0], wc.at[0, 1], lambda: order.work(4.0))
     sums_end(0)
 
     def give(m):
@@ -1063,7 +1063,7 @@
 
         lax.fori_loop(0, pairs, finish_frames, 0)
         give(m).start()
-        order.work(2.0)
+        order.work(3.0)
     order.drain()
     for m in range(2):
         give(m).wait()

time: 223 us -> 226 us (1.013)
  Pallas kernels: 222 us -> 225 us
    pallas_call x1, Pallas kernels: 210 us -> 213 us  [whole_step(): pl.pallas_call(functools.partial(kernel, dims, steps, seqs, views), out_s...]
where the time goes in v3:
time: 226 us
  Pallas kernels  225 us (100%)
    pallas_call x1, Pallas kernels, whole_step(): pl.pallas_call(functools.partial(kernel, dims, steps, seqs, views), out_s...  213 us
    pallas_call x1, Pallas kernels, results(): pl.pallas_call(write_results, grid=(count,), in_specs=[pl.BlockSpec((256,...  11.6 us

profile of v3, /device:TPU:0, one launch (start us, length us, event | category | flops | bytes accessed | tf_op | source)
XLA Modules:
  0.0 225.6 jit_solution(6095393264839117252)
XLA Ops:
  0.6 213.3 %shard_map.127 = (bf16[2,1024,2048]{2,1,0:T(8,128)(2,1)}, bf16[2,24,24,1000]{3,2,1,0:T(8,128)(2,1)}, f32[8,2048]{1,0:T(8,128)}) custom-call(bf16[2,24,24,1000]{3,2,1,0:T(8,128)(2,1)} %frames.1, bf16[2,24,24,1000]{3,2,1,0:T(8,128)(2,1)} %grad_out.1, bf16[1,2000,2000]{2,1,0:T(8,128)(2,1)} %weights.1, f32[1,2000]{1,0:T(1,128)} %gains.1, f32[1,2000]{1,0:T(1,128)} %shifts.1, ...), custom_call_target="tpu_custom_call" | custom-call | tf_op jit(solution)/shard_map/pallas_call | solution.py:1160
  213.9 11.6 %shard_map.128 = (f32[1,2000,2000]{2,1,0:T(8,128)}, bf16[48,24,1000]{2,1,0:T(8,128)(2,1)}, f32[1,2000]{1,0:T(1,128)}, f32[1,2000]{1,0:T(1,128)}, f32[1,2000]{1,0:T(1,128)}, /*index=5*/f32[1,2]{1,0:T(1,128)}) custom-call(bf16[2048,2048]{1,0:T(8,128)(2,1)} %bitcast.3, bf16[48,24,1000]{2,1,0:T(8,128)(2,1)} %bitcast.4, f32[8,2048]{1,0:T(8,128)} %get-tuple-element.17.vectors), custom_call_target="tpu_custom_call" | custom-call | tf_op jit(solution)/shard_map/pallas_call | solution.py:1119

commit v4 on v2

--- a/solution.py
+++ b/solution.py
@@ -40,6 +40,18 @@
     for k in range(8, rows, 8):
         total = total + x[k : k + 8]
     return total
+
+
+def repeat(count, body, init, times):
+    while count % times:
+        times -= 1
+
+    def several(i, carry):
+        for j in range(times):
+            carry = body(i * times + j, carry)
+        return carry
+
+    return lax.fori_loop(0, count // times, several, init)
 
 
 def dot(a, b, dims):
@@ -135,7 +147,7 @@
 
     def add(self, k, last=False):
         rows = self.regions[0][k + 1][1]
-        size = min(rows, 32)
+        size = min(rows, 64)
         out = []
         for i in range(2):
             row, _, lane, lanes = self.regions[i][k + 1]
@@ -358,7 +370,7 @@
                 target[to, :] = jnp.concatenate([x, pad], axis=1).astype(BF16)
                 return 0
 
-            lax.fori_loop(0, pairs, place, 0)
+            repeat(pairs, place, 0, 3)
 
         @pl.when(section == 1)
         def _():
@@ -370,7 +382,7 @@
                 target[to, :] = jnp.concatenate([x[:, lead:], pad], axis=1).astype(BF16)
                 return 0
 
-            lax.fori_loop(0, pairs, place, 0)
+            repeat(pairs, place, 0, 3)
 
     def patch_heads(target, m):
         @pl.when(section == 0)
@@ -385,7 +397,7 @@
                 target[to, W - 128 :] = jnp.where(lane < 128 - lead, old, head).astype(BF16)
                 return 0
 
-            lax.fori_loop(0, pairs, place, 0)
+            repeat(pairs, place, 0, 3)
 
     def pieces(row, count, u, block, spot):
         r = pl.ds(row, count)
@@ -637,7 +649,7 @@
             return s + fold(kept), q + fold(kept * d)
 
         zero = jnp.zeros((8, W), F32)
-        s, q = lax.fori_loop(0, pairs, body, (zero, zero))
+        s, q = repeat(pairs, body, (zero, zero), 3)
         s, q = jnp.sum(s, axis=0, keepdims=True), jnp.sum(q, axis=0, keepdims=True)
         n = wide(local_counts[m], 8)
         rnd, plane, _ = slim_round(layer, m)
@@ -779,7 +791,7 @@
                 g3[0, r, lanes] = y.astype(BF16)
                 return acc + fold(y)
 
-            acc = lax.fori_loop(0, pairs, body, jnp.zeros((8, HALF), F32))
+            acc = repeat(pairs, body, jnp.zeros((8, HALF), F32), 3)
             acc = jnp.sum(acc, axis=0, keepdims=True)
             if m == 0:
                 levels[4:5, lanes] = acc
@@ -978,7 +990,7 @@
             r = pl.ds(aligned(i * (2 * seqs), 16), 2 * seqs)
             return acc + fold(wide(live[r, :], 8) * f_own[r, :].astype(F32))
 
-        acc = lax.fori_loop(0, 2 * pairs, body, jnp.zeros((8, W), F32))
+        acc = repeat(2 * pairs, body, jnp.zeros((8, W), F32), 3)
         levels[0:1, :] = jnp.sum(acc, axis=0, keepdims=True)
 
     forward_end(1, 0)
@@ -1063,7 +1075,7 @@
             staged[m, pl.ds(2 * i, 2)] = (y + straight).reshape(2, seqs, half).astype(BF16)
             return 0
 
-        lax.fori_loop(0, pairs, finish_frames, 0)
+        repeat(pairs, finish_frames, 0, 3)
         give(m).start()
         order.work(2.0)
     order.drain()

time: 223 us -> 223 us (level)
  no operation moved by 1% of the time
where the time goes in v4:
time: 223 us; the launch traced here: 222 us
  Pallas kernels  221 us (99%)
    pallas_call x1, Pallas kernels, whole_step(): pl.pallas_call(functools.partial(kernel, dims, steps, seqs, views), out_s...  210 us
    pallas_call x1, Pallas kernels, results(): pl.pallas_call(write_results, grid=(count,), in_specs=[pl.BlockSpec((256,...  11.6 us

profile of v4, /device:TPU:0, one launch (start us, length us, event | category | flops | bytes accessed | tf_op | source)
XLA Modules:
  0.0 222.3 jit_solution(9494188606071561414)
XLA Ops:
  0.6 209.9 %shard_map.127 = (bf16[2,1024,2048]{2,1,0:T(8,128)(2,1)}, bf16[2,24,24,1000]{3,2,1,0:T(8,128)(2,1)}, f32[8,2048]{1,0:T(8,128)}) custom-call(bf16[2,24,24,1000]{3,2,1,0:T(8,128)(2,1)} %frames.1, bf16[2,24,24,1000]{3,2,1,0:T(8,128)(2,1)} %grad_out.1, bf16[1,2000,2000]{2,1,0:T(8,128)(2,1)} %weights.1, f32[1,2000]{1,0:T(1,128)} %gains.1, f32[1,2000]{1,0:T(1,128)} %shifts.1, ...), custom_call_target="tpu_custom_call" | custom-call | tf_op jit(solution)/shard_map/pallas_call | solution.py:1174
  210.6 11.6 %shard_map.128 = (f32[1,2000,2000]{2,1,0:T(8,128)}, bf16[48,24,1000]{2,1,0:T(8,128)(2,1)}, f32[1,2000]{1,0:T(1,128)}, f32[1,2000]{1,0:T(1,128)}, f32[1,2000]{1,0:T(1,128)}, /*index=5*/f32[1,2]{1,0:T(1,128)}) custom-call(bf16[2048,2048]{1,0:T(8,128)(2,1)} %bitcast.3, bf16[48,24,1000]{2,1,0:T(8,128)(2,1)} %bitcast.4, f32[8,2048]{1,0:T(8,128)} %get-tuple-element.17.vectors), custom_call_target="tpu_custom_call" | custom-call | tf_op jit(solution)/shard_map/pallas_call | solution.py:1133

commit v5 on v4

--- a/solution.py
+++ b/solution.py
@@ -1029,15 +1029,20 @@
     def keep_down(r, c, y):
         p_own[r, c] = y.astype(BF16)
 
-    source_grad(keep_down, wc.at[1, 0], wr1, lambda: order.work(3.0))
+    def first_half(layer, state):
+        order.work(3.0)
+        if not state:
+            sums_middle(layer)
+            state.append(layer)
+
+    source_grad(keep_down, wc.at[1, 0], wr1, functools.partial(first_half, 1, []))
     pl.semaphore_signal(credit.at[1], inc=1, device_id=sibling, device_id_type=MESH)
-    sums_middle(1)
     backward_scan(0, 0, p_own, lambda: order.work(0.6))
     backward_stats(0, 0)
+    sums_end(1)
     backward_scan(0, 1, p_own, lambda: order.work(0.6))
     backward_stats(0, 1)
     backward_middle(0, 0)
-    sums_end(1)
     transpose(f_own)
     transpose_level(f_own, 0)
     backward_middle(0, 1)

time: 223 us -> 223 us (level)
  no operation moved by 1% of the time
where the time goes in v5:
time: 223 us; the launch traced here: 222 us
  Pallas kernels  221 us (99%)
    pallas_call x1, Pallas kernels, whole_step(): pl.pallas_call(functools.partial(kernel, dims, steps, seqs, views), out_s...  210 us
    pallas_call x1, Pallas kernels, results(): pl.pallas_call(write_results, grid=(count,), in_specs=[pl.BlockSpec((256,...  11.6 us

profile of v5, /device:TPU:0, one launch (start us, length us, event | category | flops | bytes accessed | tf_op | source)
XLA Modules:
  0.0 222.3 jit_solution(11304633687301972818)
XLA Ops:
  0.6 209.9 %shard_map.127 = (bf16[2,1024,2048]{2,1,0:T(8,128)(2,1)}, bf16[2,24,24,1000]{3,2,1,0:T(8,128)(2,1)}, f32[8,2048]{1,0:T(8,128)}) custom-call(bf16[2,24,24,1000]{3,2,1,0:T(8,128)(2,1)} %frames.1, bf16[2,24,24,1000]{3,2,1,0:T(8,128)(2,1)} %grad_out.1, bf16[1,2000,2000]{2,1,0:T(8,128)(2,1)} %weights.1, f32[1,2000]{1,0:T(1,128)} %gains.1, f32[1,2000]{1,0:T(1,128)} %shifts.1, ...), custom_call_target="tpu_custom_call" | custom-call | tf_op jit(solution)/shard_map/pallas_call | solution.py:1179
  210.5 11.6 %shard_map.128 = (f32[1,2000,2000]{2,1,0:T(8,128)}, bf16[48,24,1000]{2,1,0:T(8,128)(2,1)}, f32[1,2000]{1,0:T(1,128)}, f32[1,2000]{1,0:T(1,128)}, f32[1,2000]{1,0:T(1,128)}, /*index=5*/f32[1,2]{1,0:T(1,128)}) custom-call(bf16[2048,2048]{1,0:T(8,128)(2,1)} %bitcast.3, bf16[48,24,1000]{2,1,0:T(8,128)(2,1)} %bitcast.4, f32[8,2048]{1,0:T(8,128)} %get-tuple-element.17.vectors), custom_call_target="tpu_custom_call" | custom-call | tf_op jit(solution)/shard_map/pallas_call | solution.py:1138
